TPU v7x, 512 devices: a whole 4x8x8 slice. The times are simulated.
512 devices in a mesh: seq: 64 (over y_hi, z, x), mp: 8 (over y_lo, core).
Axes of the slice: x: 4, y: 8 (y_hi: 2, y_lo: 4; y = y_hi * 4 + y_lo), z: 8, core: 2. Of those that a mesh axis runs over, the one named last changes fastest.
Arguments:
- queries: bfloat16 [32768, 4096], P(('seq', 'mp')), may hold values from -6 to 6
- memory_keys: bfloat16 [512, 4096], P('seq', 'mp'), may hold values from -6 to 6
- memory_values: bfloat16 [512, 4096], P('seq', 'mp'), may hold values from -48 to 48
- output_grad: bfloat16 [32768, 4096], P(('seq', 'mp')), may hold values from -24 to 24
Outputs:
- attended: bfloat16 [32768, 4096], P(('seq', 'mp'))
- query_grad: bfloat16 [32768, 4096], P(('seq', 'mp'))
- key_grad: bfloat16 [512, 4096], P('seq', 'mp')
- value_grad: bfloat16 [512, 4096], P('seq', 'mp')
All inputs are finite; a program needn't handle non-finite values.
Results may differ from a plain program's by a relative error of at most 0.012.
The roundings to bfloat16 on the way count: a program that leaves them out, or rounds other values in their place, can miss the bound.
Values may be sent and summed in bfloat16 or wider, within the bound.
A program may use at most 64 MiB of HBM per device.

v0:
```python
import math

import jax
import jax.numpy as jnp
from jax import lax
from jax.sharding import PartitionSpec as P

DH = 128


def split_heads(matrix, head_width):
    row_count = matrix.shape[0]
    return matrix.reshape(row_count, -1, head_width).transpose(1, 0, 2)


def join_heads(stacked):
    head_count, row_count, head_width = stacked.shape
    return stacked.transpose(1, 0, 2).reshape(row_count, head_count * head_width)


def forward_head(operands):
    query_rows, key_rows, value_rows = operands
    temper = 1.0 / math.sqrt(query_rows.shape[1])
    scores = jnp.dot(query_rows, key_rows.T, preferred_element_type=jnp.float32) * temper
    peak_score = jnp.max(scores, axis=1, keepdims=True)
    log_total = peak_score + jnp.log(jnp.sum(jnp.exp(scores - peak_score), axis=1, keepdims=True))
    attention_weights = jnp.exp(scores - log_total).astype(jnp.bfloat16)
    attended = jnp.dot(attention_weights, value_rows, preferred_element_type=jnp.float32).astype(
        jnp.bfloat16
    )
    return (attended, log_total)


def score_gradient(query_rows, key_rows, value_rows, grad_rows, attended, log_total):
    temper = 1.0 / math.sqrt(query_rows.shape[1])
    scores = jnp.dot(query_rows, key_rows.T, preferred_element_type=jnp.float32) * temper
    exact_weights = jnp.exp(scores - log_total)
    row_delta = jnp.sum(
        grad_rows.astype(jnp.float32) * attended.astype(jnp.float32), axis=1, keepdims=True
    )
    prob_grad = jnp.dot(grad_rows, value_rows.T, preferred_element_type=jnp.float32)
    score_grad = (exact_weights * (prob_grad - row_delta) * temper).astype(jnp.bfloat16)
    return (exact_weights.astype(jnp.bfloat16), score_grad)


def backward_head(operands):
    query_rows, key_rows, value_rows, grad_rows, attended, log_total = operands
    attention_weights, score_grad = score_gradient(
        query_rows, key_rows, value_rows, grad_rows, attended, log_total
    )
    query_grad = jnp.dot(score_grad, key_rows, preferred_element_type=jnp.float32).astype(
        jnp.bfloat16
    )
    key_grad = jnp.dot(score_grad.T, query_rows, preferred_element_type=jnp.float32)
    value_grad = jnp.dot(attention_weights.T, grad_rows, preferred_element_type=jnp.float32)
    return (query_grad, key_grad, value_grad)


def shards(queries, memory_keys, memory_values, output_grad):
    local_queries, local_grad = (
        lax.all_to_all(queries, "mp", split_axis=1, concat_axis=0, tiled=True),
        lax.all_to_all(output_grad, "mp", split_axis=1, concat_axis=0, tiled=True),
    )
    keys_whole, values_whole = (
        lax.all_gather(memory_keys, "seq", axis=0, tiled=True),
        lax.all_gather(memory_values, "seq", axis=0, tiled=True),
    )
    query_heads = split_heads(local_queries, DH)
    grad_heads = split_heads(local_grad, DH)
    attended_heads, log_totals = lax.map(
        forward_head, (query_heads, split_heads(keys_whole, DH), split_heads(values_whole, DH))
    )
    keys_again, values_again = (
        lax.all_gather(memory_keys, "seq", axis=0, tiled=True),
        lax.all_gather(memory_values, "seq", axis=0, tiled=True),
    )
    key_heads = split_heads(keys_again, DH)
    value_heads = split_heads(values_again, DH)
    query_grad_heads, key_terms, value_terms = lax.map(
        backward_head, (query_heads, key_heads, value_heads, grad_heads, attended_heads, log_totals)
    )
    key_grad, value_grad = (
        lax.psum_scatter(join_heads(key_terms), "seq", scatter_dimension=0, tiled=True),
        lax.psum_scatter(join_heads(value_terms), "seq", scatter_dimension=0, tiled=True),
    )
    attended, query_grad = (
        lax.all_to_all(join_heads(attended_heads), "mp", split_axis=0, concat_axis=1, tiled=True),
        lax.all_to_all(join_heads(query_grad_heads), "mp", split_axis=0, concat_axis=1, tiled=True),
    )
    return (attended, query_grad, key_grad.astype(jnp.bfloat16), value_grad.astype(jnp.bfloat16))


def solution(mesh):
    return jax.shard_map(
        shards,
        mesh=mesh,
        in_specs=(P(("seq", "mp"), None), P("seq", "mp"), P("seq", "mp"), P(("seq", "mp"), None)),
        out_specs=(P(("seq", "mp"), None), P(("seq", "mp"), None), P("seq", "mp"), P("seq", "mp")),
        check_vma=False,
    )
```

profile of v0, /device:TPU:8, one launch (start us, length us, event | category | flops | bytes accessed | tf_op | source)
XLA Modules:
  0.0 1379.3 jit_solution(6164726642870628659)
XLA Ops:
  7.2 1.9 copy.70
  9.1 9.4 all-to-all-start
  18.4 226.5 %all_gather.8 = bf16[512,512]{1,0:T(8,128)(2,1)S(1)} all-gather(bf16[8,512]{1,0:T(8,128)(2,1)S(1)} %copy-done.1), channel_id=1, replica_groups=mesh['seq'=64,'mp'=8] {'seq'}, dimensions={0}, use_global_device_ids=true | all-gather | bytes 532480 | tf_op jit(solution)/shard_map/all_gather | solution.py:65
  244.9 0.2 copy.43
  245.1 0.3 copy.46
  245.4 0.4 copy-done.2
  245.8 215.2 %all_gather.9 = bf16[512,512]{1,0:T(8,128)(2,1)S(1)} all-gather(bf16[8,512]{1,0:T(8,128)(2,1)S(1)} %copy-done.2), channel_id=1, replica_groups=mesh['seq'=64,'mp'=8] {'seq'}, dimensions={0}, use_global_device_ids=true | all-gather | bytes 532480 | tf_op jit(solution)/shard_map/all_gather | solution.py:66
  461.0 0.2 copy.44
  461.2 0.3 copy.47
  461.5 0.8 copy-done
  462.3 0.8 copy.69
  463.1 4.9 all-to-all-start.2
  468.3 3.9 while.26
  468.3 0.3 fusion.66
  468.6 0.2 exponential_reduce_fusion.2
  468.8 0.4 fusion.67
  469.3 0.3 fusion.66
  469.6 0.2 exponential_reduce_fusion.2
  469.8 0.4 fusion.67
  470.2 0.3 fusion.66
  470.5 0.2 exponential_reduce_fusion.2
  470.8 0.4 fusion.67
  471.2 0.3 fusion.66
  471.5 0.2 exponential_reduce_fusion.2
  471.7 0.4 fusion.67
  472.2 7.9 all-to-all-done.2
  480.4 13.0 while.27
  480.4 0.3 fusion.78
  480.7 0.2 fusion.79
  480.9 0.3 fusion.80
  481.2 1.0 fusion.82
  482.3 0.3 fusion.81
  482.6 1.0 fusion.83
  483.7 0.3 fusion.78
  484.1 0.3 fusion.80
  484.5 1.0 fusion.82
  485.5 0.3 fusion.81
  485.9 1.0 fusion.83
  486.9 0.3 fusion.78
  487.4 0.3 fusion.80
  487.7 1.0 fusion.82
  488.8 0.3 fusion.81
  489.1 1.0 fusion.83
  490.1 0.3 fusion.78
  490.6 0.3 fusion.80
  491.0 1.0 fusion.82
  492.0 0.3 fusion.81
  492.3 1.0 fusion.83
  493.4 2.3 copy_bitcast_fusion.1
  495.8 2.4 copy_bitcast_fusion
  498.2 0.4 copy.55
  498.6 1.0 all_to_all.62
  499.6 6.7 all-to-all-start.3
  506.3 0.4 copy.48
  506.7 1.0 all_to_all.55
  507.7 11.2 all-to-all-done.3
  518.9 6.8 all-to-all-start.1
  525.7 0.8 copy.62
  526.5 11.9 all-to-all-done.1
  538.5 0.8 copy.61
  539.3 394.6 %reduce-scatter.3.cloned.1.call-done = f32[8,512]{1,0:T(8,128)} async-done(((f32[512,512]{1,0:T(8,128)}), f32[8,512]{1,0:T(8,128)}) %reduce-scatter.3.cloned.1.call-update) | async-done | bytes 16400 | tf_op jit(solution)/shard_map/reduce_scatter | solution.py:83
  934.0 1.3 convert_element_type.30
  935.3 435.9 %reduce-scatter.5.cloned.1.call-done = f32[8,512]{1,0:T(8,128)} async-done(((f32[512,512]{1,0:T(8,128)}), f32[8,512]{1,0:T(8,128)}) %reduce-scatter.5.cloned.1.call-update) | async-done | bytes 16400 | tf_op jit(solution)/shard_map/reduce_scatter | solution.py:84
  1371.2 1.3 convert_element_type.31
  (33 shorter events, 1.2 us)
Async XLA Ops:
  9.0 9.4 copy-start.1
  9.1 454.1 %all-to-all-start = ((bf16[64,8,512]{2,0,1:T(8,128)(2,1)}), bf16[64,8,512]{2,0,1:T(8,128)(2,1)S(1)}, u32[]{:S(2)}, u32[]{:S(2)}) async-start(bf16[64,8,512]{2,0,1:T(8,128)(2,1)} %bitcast.92), calls=%async_computation | async-start | bytes 1048576 | tf_op jit(solution)/shard_map/all_to_all | solution.py:61
  245.1 0.7 copy-start.2
  461.2 1.0 copy-start
  463.1 17.0 %all-to-all-start.2 = ((bf16[64,8,512]{2,0,1:T(8,128)(2,1)}), bf16[64,8,512]{2,0,1:T(8,128)(2,1)S(1)}, u32[]{:S(2)}, u32[]{:S(2)}) async-start(bf16[64,8,512]{2,0,1:T(8,128)(2,1)} %bitcast.91), calls=%async_computation.2 | async-start | bytes 1048576 | tf_op jit(solution)/shard_map/all_to_all | solution.py:62
  468.0 466.0 %reduce-scatter.3.cloned.1.call-start = ((), (), s32[]{:S(2)}) async-start(), calls=%async_computation.6 | async-start | bytes 1064960 | tf_op jit(solution)/shard_map/reduce_scatter | solution.py:83
  495.8 875.4 %reduce-scatter.5.cloned.1.call-start = ((), (), s32[]{:S(2)}) async-start(), calls=%async_computation.7 | async-start | bytes 1064960 | tf_op jit(solution)/shard_map/reduce_scatter | solution.py:84
  499.6 19.3 %all-to-all-start.3 = ((bf16[8,64,512]{2,1,0:T(8,128)(2,1)}), bf16[8,64,512]{2,1,0:T(8,128)(2,1)S(1)}, u32[]{:S(2)}, u32[]{:S(2)}) async-start(bf16[8,64,512]{2,1,0:T(8,128)(2,1)} %all_to_all.62), calls=%async_computation.3 | async-start | bytes 1048576 | tf_op jit(solution)/shard_map/all_to_all | solution.py:88
  518.9 19.6 %all-to-all-start.1 = ((bf16[8,64,512]{2,1,0:T(8,128)(2,1)}), bf16[8,64,512]{2,1,0:T(8,128)(2,1)S(1)}, u32[]{:S(2)}, u32[]{:S(2)}) async-start(bf16[8,64,512]{2,1,0:T(8,128)(2,1)} %all_to_all.55), calls=%async_computation.1 | async-start | bytes 1048576 | tf_op jit(solution)/shard_map/all_to_all | solution.py:87
Sparse Core Ops, SparseCore 0:
  495.9 438.0 reduce-scatter.2
  937.0 434.1 reduce-scatter.4
where the time goes:
time: 1380 us
  waiting for transfers between devices  862 us (62%)
  blocking collectives  442 us (32%)
  starting transfers between devices  27.7 us (2%)
  matrix products  15.2 us (1%)
  local copies, waits for them, and re-layouts  14.7 us (1%)
  between operations  14.1 us (1%)
    reduce_scatter x1, waiting for transfers between devices, shards(): lax.psum_scatter(join_heads(value_terms), 'seq', scatter_dimension=0, til...  436 us
    reduce_scatter x1, waiting for transfers between devices, shards(): lax.psum_scatter(join_heads(key_terms), 'seq', scatter_dimension=0, tiled...  395 us
    all_gather x1, blocking collectives, shards(): lax.all_gather(memory_keys, 'seq', axis=0, tiled=True)  226 us
    all_gather x1, blocking collectives, shards(): lax.all_gather(memory_values, 'seq', axis=0, tiled=True)  215 us
  transfers between devices with their start and end apart: 6, of which 5 were waited for; matrix products, arithmetic and copies ran while one was open for 1% of the time, Pallas kernels for 0%

commit v1 on v0

v1 whole, which is shorter than its diff:
```python
import math

import jax
import jax.numpy as jnp
from jax import lax
from jax.experimental import pallas as pl
from jax.experimental.pallas import tpu as pltpu
from jax.sharding import PartitionSpec as P

MESH = pl.DeviceIdType.MESH
DH = 128
TEMPER = 1.0 / math.sqrt(DH)
LOG2E = 1.0 / math.log(2.0)
NT = (((1,), (1,)), ((), ()))
BF16, F32 = jnp.bfloat16, jnp.float32
TILES, PER_TILE, TOKENS = 4, 4, 64
TILE = PER_TILE * TOKENS


def place():
    seq, mp = lax.axis_index("seq"), lax.axis_index("mp")
    return seq % 4, (seq // 32) * 4 + mp // 2, (seq // 4) % 8, mp % 2


def device(x, y, z, core):
    return (y // 4) * 32 + z * 4 + x, (y % 4) * 2 + core


def kernel(
    q, k, v, g, att, dq, kg, vg,
    qb, gb, kvsrc, kv, attb, dqb, kc, vc, kt, vt, dk, dv, part, own, landf, landh, red, landb,
    in_send, in_recv, loc, kv1_send, kv1_recv, kv2_send, kv2_recv, out_send, out_recv,
    a_send, a_recv, b_send, b_recv,
):
    x, y, z, core = place()
    yh, a = y // 4, y % 4
    zp, zb = z // 2, z % 2
    pair = 4 * x + 2 * core + zb
    on_diagonal = x == a

    def group(i, sign):
        dx, dz, dc = i // 4, (i // 2) % 2, i % 2
        xx, bb, cc = (x + sign * dx + 4) % 4, (zb + dz) % 2, (core + dc) % 2
        return device(xx, y, 2 * zp + bb, cc), 4 * xx + 2 * cc + bb

    def across(i):
        return i // 8, i % 8, device(a, (i // 8) * 4 + x, i % 8, core)

    def along(d):
        return device(x, (y + d + 8) % 8, z, core)

    def remote(src, dst, send, recv, to):
        return pltpu.make_async_remote_copy(
            src_ref=src, dst_ref=dst, send_sem=send, recv_sem=recv, device_id=to, device_id_type=MESH
        )

    def bytes_of(ref, sem):
        pltpu.make_async_copy(ref, ref, sem).wait()

    def is_me(i):
        return on_diagonal & (i // 8 == yh) & (i % 8 == z)

    def columns(head_pair, head):
        return pl.ds(pl.multiple_of(head_pair * 256 + head * 128, 128), 128)

    barrier = pltpu.get_barrier_semaphore()

    def greet(to):
        pl.semaphore_signal(barrier, inc=1, device_id=to, device_id_type=MESH)

    @pl.loop(0, 16)
    def _(i):
        @pl.when(jnp.logical_not(is_me(i)))
        def _():
            greet(across(i)[2])

    @pl.loop(1, 16)
    def _(i):
        greet(group(i, 1)[0])

    for d in (1, -1, 2, -2):
        greet(along(d))

    mine = []
    for h in range(2):
        for n, (src, dst) in enumerate(((q, qb), (g, gb))):
            mine.append(pltpu.make_async_copy(src.at[:, columns(pair, h)], dst.at[h, 0], loc.at[n, h]))
            mine[-1].start()
    for h in range(4):
        kvsrc[h] = jnp.concatenate(
            [k[:, h * DH : (h + 1) * DH].astype(F32), v[:, h * DH : (h + 1) * DH].astype(F32)], axis=0
        ).astype(BF16)

    pl.semaphore_wait(barrier, 35 - on_diagonal.astype(jnp.int32))

    @pl.loop(0, 16)
    def _(i):
        h, zz, to = across(i)
        half = kvsrc.at[pl.ds((zz % 2) * 2, 2)]
        dst = kv.at[:, x, yh * 8 + z]

        @pl.when(jnp.logical_not(is_me(i)))
        def _():
            remote(half, dst, kv1_send, kv1_recv, to).start()

        @pl.when(is_me(i))
        def _():
            copy = pltpu.make_async_copy(half, dst, loc.at[2, 0])
            copy.start()
            copy.wait()

    for h in range(2):
        for t in range(TILES):
            for i in range(max(1, t * PER_TILE), (t + 1) * PER_TILE):
                to, theirs = group(i, 1)
                for n, (src, dst) in enumerate(((q, qb), (g, gb))):
                    remote(src.at[:, columns(theirs, h)], dst.at[h, i], in_send, in_recv.at[h, t, n], to).start()

    @pl.when(on_diagonal)
    def _():
        bytes_of(kv.at[:, 0, pl.ds(0, 15)], kv1_recv)

    @pl.when(jnp.logical_not(on_diagonal))
    def _():
        bytes_of(kv.at[:, 0], kv1_recv)

    lower, upper = pl.ds(0, 8), pl.ds(8, 8)
    for h in range(2):
        for piece, d in ((pl.ds(0, 16), 1), (pl.ds(0, 16), -1), (lower, 2), (upper, -2)):
            ref = kv.at[h, a, piece]
            remote(ref, ref, kv2_send, kv2_recv.at[h], along(d)).start()

    for h in range(2):
        bytes_of(kv.at[h, pl.ds(0, 3)], kv2_recv.at[h])
        both = kv[h].reshape(64, 16, DH).astype(F32)
        keys = both[:, :8].reshape(512, DH)
        values = both[:, 8:].reshape(512, DH)
        kc[...] = keys.astype(BF16)
        vc[...] = values.astype(BF16)
        kt[...] = keys.T.astype(BF16)
        vt[...] = values.T.astype(BF16)
        for copy in mine[2 * h : 2 * h + 2]:
            copy.wait()
        for t in range(TILES):
            for n, dst in enumerate((qb, gb)):
                bytes_of(dst.at[h, pl.ds(0, 3 if t == 0 else 4)], in_recv.at[h, t, n])
            rows = pl.ds(t * PER_TILE, PER_TILE)
            qt = qb[h, rows].reshape(TILE, DH)
            gt = gb[h, rows].reshape(TILE, DH)
            s = lax.dot_general(kc[...], qt, NT, preferred_element_type=F32)
            dp = lax.dot_general(vc[...], gt, NT, preferred_element_type=F32)
            top = jnp.max(s, axis=0, keepdims=True)
            e = jnp.exp2((s - top) * (TEMPER * LOG2E))
            inverse = 1.0 / jnp.sum(e, axis=0, keepdims=True)
            delta = jnp.sum(e * dp, axis=0, keepdims=True) * inverse
            p = (e * inverse).astype(BF16)
            ds = (e * (dp - delta) * (inverse * TEMPER)).astype(BF16)
            attb[h, rows] = (
                jnp.dot(vt[...], p, preferred_element_type=F32).T.astype(BF16).reshape(PER_TILE, TOKENS, DH)
            )
            dqb[h, rows] = (
                jnp.dot(kt[...], ds, preferred_element_type=F32).T.astype(BF16).reshape(PER_TILE, TOKENS, DH)
            )
            for i in range(t * PER_TILE, (t + 1) * PER_TILE):
                for n, (src, dst) in enumerate(((attb, att), (dqb, dq))):
                    target = dst.at[:, columns(pair, h)]
                    if i:
                        remote(src.at[h, i], target, out_send, out_recv.at[n], group(i, -1)[0]).start()
                    else:
                        pltpu.make_async_copy(src.at[h, i], target, loc.at[n, 2 + h]).start()
            dk_t = jnp.dot(ds, qt, preferred_element_type=F32)
            dv_t = jnp.dot(p, gt, preferred_element_type=F32)
            if t == 0:
                dk[...] = dk_t
                dv[...] = dv_t
            else:
                dk[...] += dk_t
                dv[...] += dv_t
        whole = jnp.concatenate([dk[...].reshape(64, 8, DH), dv[...].reshape(64, 8, DH)], axis=1)
        own[h] = whole.reshape(4, 16, 16, DH)
        part[h] = whole.astype(BF16).reshape(4, 16, 16, DH)
        for n, d in enumerate((1, -1)):
            remote(part.at[h, (a + d + 4) % 4], landf.at[h, n], a_send, a_recv.at[h, 0], along(d)).start()
        for n, d in enumerate((-2, 2)):
            remote(
                part.at[h, (a + 2) % 4, pl.ds(n * 8, 8)], landh.at[h, n], a_send, a_recv.at[h, 1], along(d)
            ).start()

    for h in range(2):
        bytes_of(landf.at[h], a_recv.at[h, 0])
        bytes_of(landh.at[h], a_recv.at[h, 1])
        total = own[h, a] + landf[h, 0].astype(F32) + landf[h, 1].astype(F32)
        total += landh[h].astype(F32).reshape(16, 16, DH)
        red[:, h] = total.astype(BF16)

        @pl.loop(0, 16)
        def _(i):
            hh, zz, to = across(i)
            dst = landb.at[yh * 4 + zp, zb * 2 + h]

            @pl.when(jnp.logical_not(is_me(i)))
            def _():
                remote(red.at[i, h], dst, b_send, b_recv, to).start()

            @pl.when(is_me(i))
            def _():
                copy = pltpu.make_async_copy(red.at[i, h], dst, loc.at[2, 1])
                copy.start()
                copy.wait()

    for n, (src, dst) in enumerate(((attb, att), (dqb, dq))):
        for h in range(2):
            pltpu.make_async_copy(src.at[h, 0], dst.at[:, columns(pair, h)], loc.at[n, 2 + h]).wait()

    for sem in (b_recv, b_send):

        @pl.when(on_diagonal)
        def _():
            bytes_of(red.at[pl.ds(0, 15)], sem)

        @pl.when(jnp.logical_not(on_diagonal))
        def _():
            bytes_of(red, sem)

    final = landb[0].astype(F32)
    for n in range(1, 8):
        final += landb[n].astype(F32)
    for h in range(4):
        kg[:, h * DH : (h + 1) * DH] = final[h, :8].astype(BF16)
        vg[:, h * DH : (h + 1) * DH] = final[h, 8:].astype(BF16)

    for n in range(2):
        bytes_of(attb.at[:, pl.ds(0, 15)], out_recv.at[n])
        bytes_of(attb.at[:, pl.ds(0, 15)], out_send)
        bytes_of(qb.at[:, pl.ds(0, 15)], in_send)
        bytes_of(kv.at[0, pl.ds(0, 3)], kv2_send)
        bytes_of(kv.at[0, pl.ds(0, 3)], a_send)

    @pl.when(on_diagonal)
    def _():
        bytes_of(kv.at[:, 0, pl.ds(0, 15)], kv1_send)

    @pl.when(jnp.logical_not(on_diagonal))
    def _():
        bytes_of(kv.at[:, 0], kv1_send)


def shards(queries, memory_keys, memory_values, output_grad):
    vmem, hbm = pl.BlockSpec(memory_space=pltpu.VMEM), pl.BlockSpec(memory_space=pl.ANY)
    tokens, memory = jax.ShapeDtypeStruct((64, 4096), BF16), jax.ShapeDtypeStruct((8, 512), BF16)
    dma = pltpu.SemaphoreType.DMA
    return pl.pallas_call(
        kernel,
        name="attention",
        out_shape=(tokens, tokens, memory, memory),
        in_specs=[hbm, vmem, vmem, hbm],
        out_specs=(hbm, hbm, vmem, vmem),
        scratch_shapes=[
            pltpu.VMEM((2, 16, TOKENS, DH), BF16),
            pltpu.VMEM((2, 16, TOKENS, DH), BF16),
            pltpu.VMEM((4, 16, DH), BF16),
            pltpu.VMEM((2, 4, 16, 16, DH), BF16),
            pltpu.VMEM((2, 16, TOKENS, DH), BF16),
            pltpu.VMEM((2, 16, TOKENS, DH), BF16),
            pltpu.VMEM((512, DH), BF16),
            pltpu.VMEM((512, DH), BF16),
            pltpu.VMEM((DH, 512), BF16),
            pltpu.VMEM((DH, 512), BF16),
            pltpu.VMEM((512, DH), F32),
            pltpu.VMEM((512, DH), F32),
            pltpu.VMEM((2, 4, 16, 16, DH), BF16),
            pltpu.VMEM((2, 4, 16, 16, DH), F32),
            pltpu.VMEM((2, 2, 16, 16, DH), BF16),
            pltpu.VMEM((2, 2, 8, 16, DH), BF16),
            pltpu.VMEM((16, 2, 16, DH), BF16),
            pltpu.VMEM((8, 4, 16, DH), BF16),
            dma,
            dma((2, TILES, 2)),
            dma((3, 4)),
            dma,
            dma,
            dma,
            dma((2,)),
            dma,
            dma((2,)),
            dma,
            dma((2, 2)),
            dma,
            dma,
        ],
        compiler_params=pltpu.CompilerParams(
            collective_id=0, has_side_effects=True, vmem_limit_bytes=40 * 2**20
        ),
    )(queries, memory_keys, memory_values, output_grad)


def solution(mesh):
    return jax.shard_map(
        shards,
        mesh=mesh,
        in_specs=(P(("seq", "mp"), None), P("seq", "mp"), P("seq", "mp"), P(("seq", "mp"), None)),
        out_specs=(P(("seq", "mp"), None), P(("seq", "mp"), None), P("seq", "mp"), P("seq", "mp")),
        check_vma=False,
    )
```

time: 1380 us -> 74.3 us (0.05)
  the two profiles are of different devices: /device:TPU:8 before, /device:TPU:1 now
where the time goes in v1:
time: 74.3 us; the launch traced here: 74 us
  Pallas kernels  67.1 us (90%)
  local copies, waits for them, and re-layouts  6.25 us (8%)
    pallas_call x1, Pallas kernels, shards(): pl.pallas_call(kernel, name='attention', out_shape=(tokens, tokens, memor...  67.1 us
    unnamed x12, local copies, waits for them, and re-layouts  6.25 us

profile of v1, /device:TPU:1, one launch (start us, length us, event | category | flops | bytes accessed | tf_op | source)
XLA Modules:
  0.0 74.0 jit_solution(6198941539473136778)
XLA Ops:
  0.6 0.0 copy-start
  0.6 1.0 %copy-done = bf16[64,4096]{1,0:T(8,128)(2,1)S(1)} copy-done((bf16[64,4096]{1,0:T(8,128)(2,1)S(1)}, bf16[64,4096]{1,0:T(8,128)(2,1)}, u32[]{:S(2)}) %copy-start) | copy-done | bytes 524312
  1.7 0.0 copy-start.1
  1.7 1.0 %copy-done.1 = bf16[64,4096]{1,0:T(8,128)(2,1)S(1)} copy-done((bf16[64,4096]{1,0:T(8,128)(2,1)S(1)}, bf16[64,4096]{1,0:T(8,128)(2,1)}, u32[]{:S(2)}) %copy-start.1) | copy-done | bytes 524312
  2.7 0.0 copy-start.2
  2.7 0.7 copy-done.2
  3.4 0.0 copy-start.3
  3.4 0.7 copy-done.3
  4.1 67.1 %attention.1 = (bf16[64,4096]{1,0:T(8,128)(2,1)S(1)}, bf16[64,4096]{1,0:T(8,128)(2,1)S(1)}, bf16[8,512]{1,0:T(8,128)(2,1)S(1)}, bf16[8,512]{1,0:T(8,128)(2,1)S(1)}) custom-call(bf16[64,4096]{1,0:T(8,128)(2,1)S(1)} %copy-done, bf16[8,512]{1,0:T(8,128)(2,1)S(1)} %copy-done.2, bf16[8,512]{1,0:T(8,128)(2,1)S(1)} %copy-done.3, bf16[64,4096]{1,0:T(8,128)(2,1)S(1)} %copy-done.1), custom_call_target="tpu_custom_call" | custom-call | tf_op jit(solution)/shard_map/attention/pallas_call | solution.py:252
  71.2 0.8 %copy.12 = bf16[64,4096]{1,0:T(8,128)(2,1)} copy(bf16[64,4096]{1,0:T(8,128)(2,1)S(1)} %get-tuple-element.8) | data formatting | bytes 1048576
  72.0 0.8 %copy.13 = bf16[64,4096]{1,0:T(8,128)(2,1)} copy(bf16[64,4096]{1,0:T(8,128)(2,1)S(1)} %get-tuple-element.9) | data formatting | bytes 1048576
  72.8 0.6 copy.14
  73.4 0.6 copy.15
Async XLA Ops:
  0.6 1.0 %copy-start = (bf16[64,4096]{1,0:T(8,128)(2,1)S(1)}, bf16[64,4096]{1,0:T(8,128)(2,1)}, u32[]{:S(2)}) copy-start(bf16[64,4096]{1,0:T(8,128)(2,1)} %q.1) | copy-start | bytes 1572868
  1.7 1.0 %copy-start.1 = (bf16[64,4096]{1,0:T(8,128)(2,1)S(1)}, bf16[64,4096]{1,0:T(8,128)(2,1)}, u32[]{:S(2)}) copy-start(bf16[64,4096]{1,0:T(8,128)(2,1)} %g.1) | copy-start | bytes 1572868
  2.7 0.7 copy-start.2
  3.4 0.7 copy-start.3

commit v2 on v1

--- a/solution.py
+++ b/solution.py
@@ -27,24 +27,31 @@
 
 
 def kernel(
-    q, k, v, g, att, dq, kg, vg,
-    qb, gb, kvsrc, kv, attb, dqb, kc, vc, kt, vt, dk, dv, part, own, landf, landh, red, landb,
+    q, keys_in, values_in, g, att, dq, landb,
+    k, v, qb, gb, kvsrc, kv, attb, dqb, kc, vc, kt, vt, dk, dv, part, own, landf, landh, red,
     in_send, in_recv, loc, kv1_send, kv1_recv, kv2_send, kv2_recv, out_send, out_recv,
     a_send, a_recv, b_send, b_recv,
 ):
     x, y, z, core = place()
     yh, a = y // 4, y % 4
     zp, zb = z // 2, z % 2
-    pair = 4 * x + 2 * core + zb
-    on_diagonal = x == a
+    block = (x + 4 - zp) % 4
+    pair = 4 * block + 2 * core + zb
+    place_in_block = (x + z) % 4
+    to_itself = (block == a) & (place_in_block == a)
 
     def group(i, sign):
         dx, dz, dc = i // 4, (i // 2) % 2, i % 2
         xx, bb, cc = (x + sign * dx + 4) % 4, (zb + dz) % 2, (core + dc) % 2
-        return device(xx, y, 2 * zp + bb, cc), 4 * xx + 2 * cc + bb
-
-    def across(i):
-        return i // 8, i % 8, device(a, (i // 8) * 4 + x, i % 8, core)
+        return device(xx, y, 2 * zp + bb, cc), 4 * ((xx + 4 - zp) % 4) + 2 * cc + bb
+
+    def workers(i):
+        h, zz = i // 8, i % 8
+        return zz % 2, device((a + zz // 2) % 4, 4 * h + place_in_block, zz, core)
+
+    def owners(i):
+        h, zz = i // 8, i % 8
+        return device((a + 8 - zz) % 4, 4 * h + block, zz, core)
 
     def along(d):
         return device(x, (y + d + 8) % 8, z, core)
@@ -58,7 +65,7 @@
         pltpu.make_async_copy(ref, ref, sem).wait()
 
     def is_me(i):
-        return on_diagonal & (i // 8 == yh) & (i % 8 == z)
+        return to_itself & (i // 8 == yh) & (i % 8 == z)
 
     def columns(head_pair, head):
         return pl.ds(pl.multiple_of(head_pair * 256 + head * 128, 128), 128)
@@ -67,12 +74,19 @@
 
     def greet(to):
         pl.semaphore_signal(barrier, inc=1, device_id=to, device_id_type=MESH)
+
+    memory = [
+        pltpu.make_async_copy(src, dst, loc.at[2, n + 2]) for n, (src, dst) in enumerate(((keys_in, k), (values_in, v)))
+    ]
+    for copy in memory:
+        copy.start()
 
     @pl.loop(0, 16)
     def _(i):
         @pl.when(jnp.logical_not(is_me(i)))
         def _():
-            greet(across(i)[2])
+            greet(workers(i)[1])
+            greet(owners(i))
 
     @pl.loop(1, 16)
     def _(i):
@@ -86,18 +100,20 @@
         for n, (src, dst) in enumerate(((q, qb), (g, gb))):
             mine.append(pltpu.make_async_copy(src.at[:, columns(pair, h)], dst.at[h, 0], loc.at[n, h]))
             mine[-1].start()
+    for copy in memory:
+        copy.wait()
     for h in range(4):
         kvsrc[h] = jnp.concatenate(
             [k[:, h * DH : (h + 1) * DH].astype(F32), v[:, h * DH : (h + 1) * DH].astype(F32)], axis=0
         ).astype(BF16)
 
-    pl.semaphore_wait(barrier, 35 - on_diagonal.astype(jnp.int32))
+    pl.semaphore_wait(barrier, 51 - 2 * to_itself.astype(jnp.int32))
 
     @pl.loop(0, 16)
     def _(i):
-        h, zz, to = across(i)
-        half = kvsrc.at[pl.ds((zz % 2) * 2, 2)]
-        dst = kv.at[:, x, yh * 8 + z]
+        j, to = workers(i)
+        half = kvsrc.at[pl.ds(j * 2, 2)]
+        dst = kv.at[:, place_in_block, yh * 8 + z]
 
         @pl.when(jnp.logical_not(is_me(i)))
         def _():
@@ -116,11 +132,11 @@
                 for n, (src, dst) in enumerate(((q, qb), (g, gb))):
                     remote(src.at[:, columns(theirs, h)], dst.at[h, i], in_send, in_recv.at[h, t, n], to).start()
 
-    @pl.when(on_diagonal)
+    @pl.when(to_itself)
     def _():
         bytes_of(kv.at[:, 0, pl.ds(0, 15)], kv1_recv)
 
-    @pl.when(jnp.logical_not(on_diagonal))
+    @pl.when(jnp.logical_not(to_itself))
     def _():
         bytes_of(kv.at[:, 0], kv1_recv)
 
@@ -195,12 +211,11 @@
 
         @pl.loop(0, 16)
         def _(i):
-            hh, zz, to = across(i)
             dst = landb.at[yh * 4 + zp, zb * 2 + h]
 
             @pl.when(jnp.logical_not(is_me(i)))
             def _():
-                remote(red.at[i, h], dst, b_send, b_recv, to).start()
+                remote(red.at[i, h], dst, b_send, b_recv, owners(i)).start()
 
             @pl.when(is_me(i))
             def _():
@@ -214,48 +229,59 @@
 
     for sem in (b_recv, b_send):
 
-        @pl.when(on_diagonal)
+        @pl.when(to_itself)
         def _():
             bytes_of(red.at[pl.ds(0, 15)], sem)
 
-        @pl.when(jnp.logical_not(on_diagonal))
+        @pl.when(jnp.logical_not(to_itself))
         def _():
             bytes_of(red, sem)
 
+    for n in range(2):
+        bytes_of(attb.at[:, pl.ds(0, 15)], out_recv.at[n])
+        bytes_of(attb.at[:, pl.ds(0, 15)], out_send)
+        bytes_of(qb.at[:, pl.ds(0, 15)], in_send)
+        bytes_of(kv.at[0, pl.ds(0, 3)], kv2_send)
+        bytes_of(kv.at[0, pl.ds(0, 3)], a_send)
+
+    @pl.when(to_itself)
+    def _():
+        bytes_of(kv.at[:, 0, pl.ds(0, 15)], kv1_send)
+
+    @pl.when(jnp.logical_not(to_itself))
+    def _():
+        bytes_of(kv.at[:, 0], kv1_send)
+
+
+def finish(att_in, dq_in, landb, att, dq, kg, vg, sems):
+    copies = [
+        pltpu.make_async_copy(src, dst, sems.at[n]) for n, (src, dst) in enumerate(((att_in, att), (dq_in, dq)))
+    ]
+    for copy in copies:
+        copy.start()
     final = landb[0].astype(F32)
     for n in range(1, 8):
         final += landb[n].astype(F32)
     for h in range(4):
         kg[:, h * DH : (h + 1) * DH] = final[h, :8].astype(BF16)
         vg[:, h * DH : (h + 1) * DH] = final[h, 8:].astype(BF16)
-
-    for n in range(2):
-        bytes_of(attb.at[:, pl.ds(0, 15)], out_recv.at[n])
-        bytes_of(attb.at[:, pl.ds(0, 15)], out_send)
-        bytes_of(qb.at[:, pl.ds(0, 15)], in_send)
-        bytes_of(kv.at[0, pl.ds(0, 3)], kv2_send)
-        bytes_of(kv.at[0, pl.ds(0, 3)], a_send)
-
-    @pl.when(on_diagonal)
-    def _():
-        bytes_of(kv.at[:, 0, pl.ds(0, 15)], kv1_send)
-
-    @pl.when(jnp.logical_not(on_diagonal))
-    def _():
-        bytes_of(kv.at[:, 0], kv1_send)
+    for copy in copies:
+        copy.wait()
 
 
 def shards(queries, memory_keys, memory_values, output_grad):
     vmem, hbm = pl.BlockSpec(memory_space=pltpu.VMEM), pl.BlockSpec(memory_space=pl.ANY)
     tokens, memory = jax.ShapeDtypeStruct((64, 4096), BF16), jax.ShapeDtypeStruct((8, 512), BF16)
     dma = pltpu.SemaphoreType.DMA
-    return pl.pallas_call(
+    att, dq, landb = pl.pallas_call(
         kernel,
         name="attention",
-        out_shape=(tokens, tokens, memory, memory),
-        in_specs=[hbm, vmem, vmem, hbm],
-        out_specs=(hbm, hbm, vmem, vmem),
+        out_shape=(pltpu.VMEM((64, 4096), BF16), pltpu.VMEM((64, 4096), BF16), pltpu.VMEM((8, 4, 16, DH), BF16)),
+        in_specs=[hbm] * 4,
+        out_specs=(vmem, vmem, vmem),
         scratch_shapes=[
+            pltpu.VMEM((8, 512), BF16),
+            pltpu.VMEM((8, 512), BF16),
             pltpu.VMEM((2, 16, TOKENS, DH), BF16),
             pltpu.VMEM((2, 16, TOKENS, DH), BF16),
             pltpu.VMEM((4, 16, DH), BF16),
@@ -273,7 +299,6 @@
             pltpu.VMEM((2, 2, 16, 16, DH), BF16),
             pltpu.VMEM((2, 2, 8, 16, DH), BF16),
             pltpu.VMEM((16, 2, 16, DH), BF16),
-            pltpu.VMEM((8, 4, 16, DH), BF16),
             dma,
             dma((2, TILES, 2)),
             dma((3, 4)),
@@ -289,9 +314,17 @@
             dma,
         ],
         compiler_params=pltpu.CompilerParams(
-            collective_id=0, has_side_effects=True, vmem_limit_bytes=40 * 2**20
+            collective_id=0, has_side_effects=True, vmem_limit_bytes=60 * 2**20
         ),
     )(queries, memory_keys, memory_values, output_grad)
+    return pl.pallas_call(
+        finish,
+        name="finish",
+        out_shape=(tokens, tokens, memory, memory),
+        in_specs=[vmem, vmem, vmem],
+        out_specs=(hbm, hbm, vmem, vmem),
+        scratch_shapes=[dma((2,))],
+    )(*(pltpu.with_memory_space_constraint(t, pltpu.VMEM) for t in (att, dq, landb)))
 
 
 def solution(mesh):

time: 74.3 us -> 58.3 us (0.78)
  Pallas kernels: 67.1 us -> 57.5 us
  local copies, waits for them, and re-layouts: 6.25 us -> 0 us
    pallas_call x1 -> x2, Pallas kernels: 67.1 us -> 57.5 us  [the longest x1 55.9 us: shards(): pl.pallas_call(kernel, name='attention', out_shape=(pltpu.VMEM((64, 4096)...]
    unnamed x12 -> x0, local copies, waits for them, and re-layouts: 6.25 us -> none
where the time goes in v2:
time: 58.3 us; the launch traced here: 58.1 us
  Pallas kernels  57.5 us (99%)
  between operations  0.64 us (1%)
    pallas_call x1, Pallas kernels, shards(): pl.pallas_call(kernel, name='attention', out_shape=(pltpu.VMEM((64, 4096)...  55.9 us
    pallas_call x1, Pallas kernels, shards(): pl.pallas_call(finish, name='finish', out_shape=(tokens, tokens, memory,...  1.59 us

profile of v2, /device:TPU:1, one launch (start us, length us, event | category | flops | bytes accessed | tf_op | source)
XLA Modules:
  0.0 58.1 jit_solution(1358586927346333364)
XLA Ops:
  0.6 55.9 %attention.1 = (bf16[64,4096]{1,0:T(8,128)(2,1)S(1)}, bf16[64,4096]{1,0:T(8,128)(2,1)S(1)}, bf16[8,4,16,128]{3,2,1,0:T(8,128)(2,1)S(1)}) custom-call(bf16[64,4096]{1,0:T(8,128)(2,1)} %q.1, bf16[8,512]{1,0:T(8,128)(2,1)} %keys_in.1, bf16[8,512]{1,0:T(8,128)(2,1)} %values_in.1, bf16[64,4096]{1,0:T(8,128)(2,1)} %g.1), custom_call_target="tpu_custom_call" | custom-call | tf_op jit(solution)/shard_map/attention/pallas_call | solution.py:276
  56.6 1.6 %finish.1 = (bf16[64,4096]{1,0:T(8,128)(2,1)}, bf16[64,4096]{1,0:T(8,128)(2,1)}, bf16[8,512]{1,0:T(8,128)(2,1)}, bf16[8,512]{1,0:T(8,128)(2,1)}) custom-call(bf16[64,4096]{1,0:T(8,128)(2,1)S(1)} %get-tuple-element.7.att_in, bf16[64,4096]{1,0:T(8,128)(2,1)S(1)} %get-tuple-element.8.dq_in, bf16[8,4,16,128]{3,2,1,0:T(8,128)(2,1)S(1)} %get-tuple-element.9.landb), custom_call_target="tpu_custom_call" | custom-call | tf_op jit(solution)/shard_map/finish/pallas_call | solution.py:320

commit v3 on v2

v3 whole, which is shorter than its diff:
```python
import math

import jax
import jax.numpy as jnp
from jax import lax
from jax.experimental import pallas as pl
from jax.experimental.pallas import tpu as pltpu
from jax.sharding import PartitionSpec as P

MESH = pl.DeviceIdType.MESH
DH = 128
TEMPER = 1.0 / math.sqrt(DH)
LOG2E = 1.0 / math.log(2.0)
NT = (((1,), (1,)), ((), ()))
BF16, F32 = jnp.bfloat16, jnp.float32
TILES, PER_TILE, TOKENS = 2, 8, 64
SELF = 12
TILE = PER_TILE * TOKENS


def place():
    seq, mp = lax.axis_index("seq"), lax.axis_index("mp")
    return seq % 4, (seq // 32) * 4 + mp // 2, (seq // 4) % 8, mp % 2


def device(x, y, z, core):
    return (y // 4) * 32 + z * 4 + x, (y % 4) * 2 + core


def kernel(
    q, keys_in, values_in, g, att, dq, landb,
    k, v, qb, gb, kvsrc, kv, attb, dqb, kc, vc, kt, vt, pb, dsb, part, own, landf, landh, red,
    in_send, in_recv, loc, kv1_send, kv1_recv, kv2_send, kv2_recv, out_send, out_recv,
    a_send, a_recv, b_send, b_recv,
):
    x, y, z, core = place()
    yh, a = y // 4, y % 4
    zp, zb = z // 2, z % 2
    block = (x + 4 - zp) % 4
    pair = 4 * block + 2 * core + zb
    place_in_block = (x + z) % 4
    to_itself = (block == a) & (place_in_block == a)

    def group(t, k, sign):
        odd, m = k % 2, k // 2 + (k % 2) * t
        dx = 1 + 2 * odd if t == 0 else 2 - 2 * odd
        dz, dc = m // 2, m % 2
        xx, bb, cc = (x + sign * dx + 4) % 4, (zb + dz) % 2, (core + dc) % 2
        return t * PER_TILE + odd * 4 + m, device(xx, y, 2 * zp + bb, cc), 4 * ((xx + 4 - zp) % 4) + 2 * cc + bb

    def workers(i):
        h, zz = i // 8, i % 8
        return zz % 2, device((a + zz // 2) % 4, 4 * h + place_in_block, zz, core)

    def owners(i):
        h, zz = i // 8, i % 8
        return device((a + 8 - zz) % 4, 4 * h + block, zz, core)

    def along(d):
        return device(x, (y + d + 8) % 8, z, core)

    def remote(src, dst, send, recv, to):
        return pltpu.make_async_remote_copy(
            src_ref=src, dst_ref=dst, send_sem=send, recv_sem=recv, device_id=to, device_id_type=MESH
        )

    def bytes_of(ref, sem):
        pltpu.make_async_copy(ref, ref, sem).wait()

    def memory_blocks(ref, sem):
        @pl.when(to_itself)
        def _():
            bytes_of(ref.at[pl.ds(0, 15)], sem)

        @pl.when(jnp.logical_not(to_itself))
        def _():
            bytes_of(ref, sem)

    def is_me(i):
        return to_itself & (i // 8 == yh) & (i % 8 == z)

    def columns(head_pair, head):
        return pl.ds(pl.multiple_of(head_pair * 256 + head * 128, 128), 128)

    barrier = pltpu.get_barrier_semaphore()

    def greet(to):
        pl.semaphore_signal(barrier, inc=1, device_id=to, device_id_type=MESH)

    memory = [
        pltpu.make_async_copy(src, dst, loc.at[2, n + 2]) for n, (src, dst) in enumerate(((keys_in, k), (values_in, v)))
    ]
    for copy in memory:
        copy.start()

    @pl.loop(0, 16)
    def _(i):
        @pl.when(jnp.logical_not(is_me(i)))
        def _():
            greet(workers(i)[1])
            greet(owners(i))

    for t in range(TILES):

        @pl.loop(0, PER_TILE - t)
        def _(k):
            greet(group(t, k, 1)[1])

    for d in (1, -1, 2, -2):
        greet(along(d))

    mine = []
    for h in range(2):
        for n, (src, dst) in enumerate(((q, qb), (g, gb))):
            mine.append(pltpu.make_async_copy(src.at[:, columns(pair, h)], dst.at[h, SELF], loc.at[n, h]))
            mine[-1].start()
    for copy in memory:
        copy.wait()
    for h in range(4):
        kvsrc[h] = jnp.concatenate(
            [k[:, h * DH : (h + 1) * DH].astype(F32), v[:, h * DH : (h + 1) * DH].astype(F32)], axis=0
        ).astype(BF16)

    pl.semaphore_wait(barrier, 51 - 2 * to_itself.astype(jnp.int32))

    for head in range(2):

        @pl.loop(0, 16)
        def _(i):
            j, to = workers(i)
            one = kvsrc.at[j * 2 + head]
            dst = kv.at[head, 0, yh * 8 + z]

            @pl.when(jnp.logical_not(is_me(i)))
            def _():
                remote(one, dst, kv1_send.at[head], kv1_recv.at[head], to).start()

            @pl.when(is_me(i))
            def _():
                copy = pltpu.make_async_copy(one, dst, loc.at[2, 0])
                copy.start()
                copy.wait()

    def share(h):
        for t in range(TILES):

            @pl.loop(0, PER_TILE - t)
            def _(k):
                i, to, theirs = group(t, k, 1)
                for n, (src, dst) in enumerate(((q, qb), (g, gb))):
                    remote(src.at[:, columns(theirs, h)], dst.at[h, i], in_send.at[n], in_recv.at[h, t, n], to).start()

    share(0)
    lower, upper = pl.ds(0, 8), pl.ds(8, 8)
    for h in range(2):
        memory_blocks(kv.at[h, 0], kv1_recv.at[h])
        if h == 1:
            bytes_of(kv.at[0, pl.ds(0, 3)], kv2_send.at[0])
        for piece, d in ((lower, 2), (upper, -2), (pl.ds(0, 16), 1), (pl.ds(0, 16), -1)):
            there = kv.at[h, (4 - d) % 4, piece]
            remote(kv.at[h, 0, piece], there, kv2_send.at[h], kv2_recv.at[h], along(d)).start()
        if h == 0:
            share(1)

    flows = ((pb, vt, attb, att), (dsb, kt, dqb, dq))

    def result(h, t, n):
        weights, other, buffer, _ = flows[n]
        made = jnp.dot(other[...], weights[t].reshape(512, TILE), preferred_element_type=F32)
        buffer[h, t * PER_TILE : (t + 1) * PER_TILE] = made.T.astype(BF16).reshape(PER_TILE, TOKENS, DH)

    def send(h, t, n):
        _, _, buffer, whole = flows[n]
        target = whole.at[:, columns(pair, h)]

        @pl.loop(0, PER_TILE - t)
        def _(k):
            i, to, _ = group(t, k, -1)
            remote(buffer.at[h, i], target, out_send.at[n], out_recv.at[n], to).start()

        if t == SELF // PER_TILE:
            pltpu.make_async_copy(buffer.at[h, SELF], target, loc.at[n, 2 + h]).start()

    for h in range(2):
        bytes_of(kv.at[h, pl.ds(1, 3)], kv2_recv.at[h])
        both = kv[h].reshape(64, 16, DH).astype(F32)
        keys = both[:, :8].reshape(512, DH)
        values = both[:, 8:].reshape(512, DH)
        kc[...] = keys.astype(BF16)
        vc[...] = values.astype(BF16)
        kt[...] = keys.T.astype(BF16)
        vt[...] = values.T.astype(BF16)
        for t in range(TILES):
            if t == SELF // PER_TILE:
                for copy in mine[2 * h : 2 * h + 2]:
                    copy.wait()
            for n, dst in enumerate((qb, gb)):
                bytes_of(dst.at[h, pl.ds(0, 7 if t == SELF // PER_TILE else 8)], in_recv.at[h, t, n])
            rows = pl.ds(t * PER_TILE, PER_TILE)
            qt = qb[h, rows].reshape(TILE, DH)
            gt = gb[h, rows].reshape(TILE, DH)
            s = lax.dot_general(kc[...], qt, NT, preferred_element_type=F32)
            dp = lax.dot_general(vc[...], gt, NT, preferred_element_type=F32)
            top = jnp.max(s, axis=0, keepdims=True)
            e = jnp.exp2((s - top) * (TEMPER * LOG2E))
            inverse = 1.0 / jnp.sum(e, axis=0, keepdims=True)
            delta = jnp.sum(e * dp, axis=0, keepdims=True) * inverse
            pb[t] = (e * inverse).astype(BF16).reshape(4, 128, TILE)
            dsb[t] = (e * (dp - delta) * (inverse * TEMPER)).astype(BF16).reshape(4, 128, TILE)
            if h == 0:
                for n in range(2):
                    result(h, t, n)
                    send(h, t, n)
        queries, grads = qb[h].reshape(16 * TOKENS, DH), gb[h].reshape(16 * TOKENS, DH)
        for d in (2, 1, 3, 0):
            dk, dv = (
                jnp.dot(weights[0, d], other[:TILE], preferred_element_type=F32)
                + jnp.dot(weights[1, d], other[TILE:], preferred_element_type=F32)
                for weights, other in ((dsb, queries), (pb, grads))
            )
            sums = jnp.concatenate([dk.reshape(16, 8, DH), dv.reshape(16, 8, DH)], axis=1)
            if d == 0:
                own[h] = sums
                continue
            part[h, d - 1] = sums.astype(BF16)
            for half in range(2):
                slots = pl.ds(half * 8, 8)
                if d == 2:
                    to, land = along(2 if half else -2), landh.at[h, half]
                else:
                    to, land = along(1 if d == 1 else -1), landf.at[h, d // 2, slots]
                remote(part.at[h, d - 1, slots], land, a_send.at[h], a_recv.at[h, half], to).start()

    def gather_sums(h, half):
        slots = pl.ds(half * 8, 8)
        bytes_of(part.at[h, :, slots], a_recv.at[h, half])
        total = own[h, slots] + landf[h, 0, slots].astype(F32) + landf[h, 1, slots].astype(F32)
        total += landh[h, half].astype(F32)
        red[h, slots] = total.astype(BF16)

        @pl.loop(half * 8, half * 8 + 8)
        def _(i):
            dst = landb.at[yh * 4 + zp, zb * 2 + h]

            @pl.when(jnp.logical_not(is_me(i)))
            def _():
                remote(red.at[h, i], dst, b_send.at[h], b_recv.at[h], owners(i)).start()

            @pl.when(is_me(i))
            def _():
                copy = pltpu.make_async_copy(red.at[h, i], dst, loc.at[2, 1])
                copy.start()
                copy.wait()

    gather_sums(0, 0)
    gather_sums(0, 1)
    for t in range(TILES):
        result(1, t, 0)
        send(1, t, 0)
    for t in range(TILES):
        result(1, t, 1)
    gather_sums(1, 0)
    gather_sums(1, 1)
    for t in range(TILES):
        send(1, t, 1)

    for n, (src, dst) in enumerate(((attb, att), (dqb, dq))):
        for h in range(2):
            pltpu.make_async_copy(src.at[h, SELF], dst.at[:, columns(pair, h)], loc.at[n, 2 + h]).wait()

    for h in range(2):
        for sem in (b_recv, b_send, kv1_send):
            memory_blocks(red.at[h], sem.at[h])

    bytes_of(kv.at[1, pl.ds(0, 3)], kv2_send.at[1])
    for n in range(2):
        bytes_of(attb.at[:, pl.ds(0, 15)], out_recv.at[n])
        bytes_of(attb.at[:, pl.ds(0, 15)], out_send.at[n])
        bytes_of(qb.at[:, pl.ds(0, 15)], in_send.at[n])
        bytes_of(part.at[n], a_send.at[n])


def finish(att_in, dq_in, landb, att, dq, kg, vg, sems):
    copies = [
        pltpu.make_async_copy(src.at[pl.ds(r * 16, 16)], dst.at[pl.ds(r * 16, 16)], sems.at[n, r])
        for r in range(4)
        for n, (src, dst) in enumerate(((att_in, att), (dq_in, dq)))
    ]
    for copy in copies:
        copy.start()
    final = landb[0].astype(F32)
    for n in range(1, 8):
        final += landb[n].astype(F32)
    for h in range(4):
        kg[:, h * DH : (h + 1) * DH] = final[h, :8].astype(BF16)
        vg[:, h * DH : (h + 1) * DH] = final[h, 8:].astype(BF16)
    for copy in copies:
        copy.wait()


def shards(queries, memory_keys, memory_values, output_grad):
    vmem, hbm = pl.BlockSpec(memory_space=pltpu.VMEM), pl.BlockSpec(memory_space=pl.ANY)
    tokens, memory = jax.ShapeDtypeStruct((64, 4096), BF16), jax.ShapeDtypeStruct((8, 512), BF16)
    dma = pltpu.SemaphoreType.DMA
    att, dq, landb = pl.pallas_call(
        kernel,
        name="attention",
        out_shape=(pltpu.VMEM((64, 4096), BF16), pltpu.VMEM((64, 4096), BF16), pltpu.VMEM((8, 4, 16, DH), BF16)),
        in_specs=[hbm] * 4,
        out_specs=(vmem, vmem, vmem),
        scratch_shapes=[
            pltpu.VMEM((8, 512), BF16),
            pltpu.VMEM((8, 512), BF16),
            pltpu.VMEM((2, 16, TOKENS, DH), BF16),
            pltpu.VMEM((2, 16, TOKENS, DH), BF16),
            pltpu.VMEM((4, 16, DH), BF16),
            pltpu.VMEM((2, 4, 16, 16, DH), BF16),
            pltpu.VMEM((2, 16, TOKENS, DH), BF16),
            pltpu.VMEM((2, 16, TOKENS, DH), BF16),
            pltpu.VMEM((512, DH), BF16),
            pltpu.VMEM((512, DH), BF16),
            pltpu.VMEM((DH, 512), BF16),
            pltpu.VMEM((DH, 512), BF16),
            pltpu.VMEM((TILES, 4, 128, TILE), BF16),
            pltpu.VMEM((TILES, 4, 128, TILE), BF16),
            pltpu.VMEM((2, 3, 16, 16, DH), BF16),
            pltpu.VMEM((2, 16, 16, DH), F32),
            pltpu.VMEM((2, 2, 16, 16, DH), BF16),
            pltpu.VMEM((2, 2, 8, 16, DH), BF16),
            pltpu.VMEM((2, 16, 16, DH), BF16),
            dma((2,)),
            dma((2, TILES, 2)),
            dma((3, 4)),
            dma((2,)),
            dma((2,)),
            dma((2,)),
            dma((2,)),
            dma((2,)),
            dma((2,)),
            dma((2,)),
            dma((2, 2)),
            dma((2,)),
            dma((2,)),
        ],
        compiler_params=pltpu.CompilerParams(
            collective_id=0, has_side_effects=True, vmem_limit_bytes=60 * 2**20
        ),
    )(queries, memory_keys, memory_values, output_grad)
    return pl.pallas_call(
        finish,
        name="finish",
        out_shape=(tokens, tokens, memory, memory),
        in_specs=[vmem, vmem, vmem],
        out_specs=(hbm, hbm, vmem, vmem),
        scratch_shapes=[dma((2, 4))],
    )(*(pltpu.with_memory_space_constraint(t, pltpu.VMEM) for t in (att, dq, landb)))


def solution(mesh):
    return jax.shard_map(
        shards,
        mesh=mesh,
        in_specs=(P(("seq", "mp"), None), P("seq", "mp"), P("seq", "mp"), P(("seq", "mp"), None)),
        out_specs=(P(("seq", "mp"), None), P(("seq", "mp"), None), P("seq", "mp"), P("seq", "mp")),
        check_vma=False,
    )
```

time: 58.3 us -> 56.3 us (0.966)
  Pallas kernels: 57.5 us -> 55.3 us
    pallas_call x1, Pallas kernels: 55.9 us -> 53.7 us  [shards(): pl.pallas_call(kernel, name='attention', out_shape=(pltpu.VMEM((64, 4096)...]
where the time goes in v3:
time: 56.3 us; the launch traced here: 55.9 us
  Pallas kernels  55.3 us (98%)
  between operations  0.64 us (1%)
    pallas_call x1, Pallas kernels, shards(): pl.pallas_call(kernel, name='attention', out_shape=(pltpu.VMEM((64, 4096)...  53.7 us
    pallas_call x1, Pallas kernels, shards(): pl.pallas_call(finish, name='finish', out_shape=(tokens, tokens, memory,...  1.63 us

profile of v3, /device:TPU:1, one launch (start us, length us, event | category | flops | bytes accessed | tf_op | source)
XLA Modules:
  0.0 55.9 jit_solution(9451432168385047550)
XLA Ops:
  0.6 53.7 %attention.1 = (bf16[64,4096]{1,0:T(8,128)(2,1)S(1)}, bf16[64,4096]{1,0:T(8,128)(2,1)S(1)}, bf16[8,4,16,128]{3,2,1,0:T(8,128)(2,1)S(1)}) custom-call(bf16[64,4096]{1,0:T(8,128)(2,1)} %q.1, bf16[8,512]{1,0:T(8,128)(2,1)} %keys_in.1, bf16[8,512]{1,0:T(8,128)(2,1)} %values_in.1, bf16[64,4096]{1,0:T(8,128)(2,1)} %g.1), custom_call_target="tpu_custom_call" | custom-call | tf_op jit(solution)/shard_map/attention/pallas_call | solution.py:305
  54.3 1.6 %finish.1 = (bf16[64,4096]{1,0:T(8,128)(2,1)}, bf16[64,4096]{1,0:T(8,128)(2,1)}, bf16[8,512]{1,0:T(8,128)(2,1)}, bf16[8,512]{1,0:T(8,128)(2,1)}) custom-call(bf16[64,4096]{1,0:T(8,128)(2,1)S(1)} %get-tuple-element.7.att_in, bf16[64,4096]{1,0:T(8,128)(2,1)S(1)} %get-tuple-element.8.dq_in, bf16[8,4,16,128]{3,2,1,0:T(8,128)(2,1)S(1)} %get-tuple-element.9.landb), custom_call_target="tpu_custom_call" | custom-call | tf_op jit(solution)/shard_map/finish/pallas_call | solution.py:349

commit v4 on v3

--- a/solution.py
+++ b/solution.py
@@ -76,6 +76,10 @@
         def _():
             bytes_of(ref, sem)
 
+    def far_first(n):
+        step = (n + 1) // 2
+        return (z + 12 + step * (2 * (n % 2) - 1)) % 8
+
     def is_me(i):
         return to_itself & (i // 8 == yh) & (i % 8 == z)
 
@@ -126,7 +130,8 @@
     for head in range(2):
 
         @pl.loop(0, 16)
-        def _(i):
+        def _(n):
+            i = ((yh + 1 + n) % 2) * 8 + far_first(n // 2)
             j, to = workers(i)
             one = kvsrc.at[j * 2 + head]
             dst = kv.at[head, 0, yh * 8 + z]
@@ -238,8 +243,9 @@
         total += landh[h, half].astype(F32)
         red[h, slots] = total.astype(BF16)
 
-        @pl.loop(half * 8, half * 8 + 8)
-        def _(i):
+        @pl.loop(0, 8)
+        def _(n):
+            i = half * 8 + far_first(n)
             dst = landb.at[yh * 4 + zp, zb * 2 + h]
 
             @pl.when(jnp.logical_not(is_me(i)))
@@ -280,20 +286,21 @@
         bytes_of(part.at[n], a_send.at[n])
 
 
-def finish(att_in, dq_in, landb, att, dq, kg, vg, sems):
+def finish(att_in, dq_in, landb, att, dq, kg, vg, kg_made, vg_made, sems):
     copies = [
-        pltpu.make_async_copy(src.at[pl.ds(r * 16, 16)], dst.at[pl.ds(r * 16, 16)], sems.at[n, r])
-        for r in range(4)
-        for n, (src, dst) in enumerate(((att_in, att), (dq_in, dq)))
+        pltpu.make_async_copy(src, dst, sems.at[n])
+        for n, (src, dst) in enumerate(((att_in, att), (dq_in, dq), (kg_made, kg), (vg_made, vg)))
     ]
-    for copy in copies:
+    for copy in copies[:2]:
         copy.start()
     final = landb[0].astype(F32)
     for n in range(1, 8):
         final += landb[n].astype(F32)
     for h in range(4):
-        kg[:, h * DH : (h + 1) * DH] = final[h, :8].astype(BF16)
-        vg[:, h * DH : (h + 1) * DH] = final[h, 8:].astype(BF16)
+        kg_made[:, h * DH : (h + 1) * DH] = final[h, :8].astype(BF16)
+        vg_made[:, h * DH : (h + 1) * DH] = final[h, 8:].astype(BF16)
+    for copy in copies[2:]:
+        copy.start()
     for copy in copies:
         copy.wait()
 
@@ -351,8 +358,8 @@
         name="finish",
         out_shape=(tokens, tokens, memory, memory),
         in_specs=[vmem, vmem, vmem],
-        out_specs=(hbm, hbm, vmem, vmem),
-        scratch_shapes=[dma((2, 4))],
+        out_specs=(hbm, hbm, hbm, hbm),
+        scratch_shapes=[pltpu.VMEM((8, 512), BF16), pltpu.VMEM((8, 512), BF16), dma((4,))],
     )(*(pltpu.with_memory_space_constraint(t, pltpu.VMEM) for t in (att, dq, landb)))
 
 

time: 56.3 us -> 55.5 us (0.986)
  Pallas kernels: 55.3 us -> 54.1 us
    pallas_call x1, Pallas kernels: 1.63 us -> 1.01 us  [shards(): pl.pallas_call(finish, name='finish', out_shape=(tokens, tokens, memory,...]
    pallas_call x1, Pallas kernels: 53.7 us -> 53.1 us  [shards(): pl.pallas_call(kernel, name='attention', out_shape=(pltpu.VMEM((64, 4096)...]
where the time goes in v4:
time: 55.5 us; the launch traced here: 54.7 us
  Pallas kernels  54.1 us (97%)
  between operations  0.64 us (1%)
    pallas_call x1, Pallas kernels, shards(): pl.pallas_call(kernel, name='attention', out_shape=(pltpu.VMEM((64, 4096)...  53.1 us

profile of v4, /device:TPU:1, one launch (start us, length us, event | category | flops | bytes accessed | tf_op | source)
XLA Modules:
  0.0 54.7 jit_solution(7818067894915542112)
XLA Ops:
  0.6 53.1 %attention.1 = (bf16[64,4096]{1,0:T(8,128)(2,1)S(1)}, bf16[64,4096]{1,0:T(8,128)(2,1)S(1)}, bf16[8,4,16,128]{3,2,1,0:T(8,128)(2,1)S(1)}) custom-call(bf16[64,4096]{1,0:T(8,128)(2,1)} %q.1, bf16[8,512]{1,0:T(8,128)(2,1)} %keys_in.1, bf16[8,512]{1,0:T(8,128)(2,1)} %values_in.1, bf16[64,4096]{1,0:T(8,128)(2,1)} %g.1), custom_call_target="tpu_custom_call" | custom-call | tf_op jit(solution)/shard_map/attention/pallas_call | solution.py:312
  53.7 1.0 %finish.1 = (bf16[64,4096]{1,0:T(8,128)(2,1)}, bf16[64,4096]{1,0:T(8,128)(2,1)}, bf16[8,512]{1,0:T(8,128)(2,1)}, bf16[8,512]{1,0:T(8,128)(2,1)}) custom-call(bf16[64,4096]{1,0:T(8,128)(2,1)S(1)} %get-tuple-element.7.att_in, bf16[64,4096]{1,0:T(8,128)(2,1)S(1)} %get-tuple-element.8.dq_in, bf16[8,4,16,128]{3,2,1,0:T(8,128)(2,1)S(1)} %get-tuple-element.9.landb), custom_call_target="tpu_custom_call" | custom-call | tf_op jit(solution)/shard_map/finish/pallas_call | solution.py:356

commit v5 on v4

--- a/solution.py
+++ b/solution.py
@@ -98,7 +98,9 @@
         copy.start()
 
     @pl.loop(0, 16)
-    def _(i):
+    def _(n):
+        i = ((yh + 1 + n) % 2) * 8 + far_first(n // 2)
+
         @pl.when(jnp.logical_not(is_me(i)))
         def _():
             greet(workers(i)[1])

time: 55.5 us -> 55.6 us (level)
  no operation moved by 1% of the time
where the time goes in v5:
time: 55.6 us; the launch traced here: 55.1 us
  Pallas kernels  54.5 us (98%)
  between operations  0.64 us (1%)
    pallas_call x1, Pallas kernels, shards(): pl.pallas_call(kernel, name='attention', out_shape=(pltpu.VMEM((64, 4096)...  53.5 us

profile of v5, /device:TPU:1, one launch (start us, length us, event | category | flops | bytes accessed | tf_op | source)
XLA Modules:
  0.0 55.1 jit_solution(1904435316304808208)
XLA Ops:
  0.6 53.5 %attention.1 = (bf16[64,4096]{1,0:T(8,128)(2,1)S(1)}, bf16[64,4096]{1,0:T(8,128)(2,1)S(1)}, bf16[8,4,16,128]{3,2,1,0:T(8,128)(2,1)S(1)}) custom-call(bf16[64,4096]{1,0:T(8,128)(2,1)} %q.1, bf16[8,512]{1,0:T(8,128)(2,1)} %keys_in.1, bf16[8,512]{1,0:T(8,128)(2,1)} %values_in.1, bf16[64,4096]{1,0:T(8,128)(2,1)} %g.1), custom_call_target="tpu_custom_call" | custom-call | tf_op jit(solution)/shard_map/attention/pallas_call | solution.py:314
  54.1 1.0 %finish.1 = (bf16[64,4096]{1,0:T(8,128)(2,1)}, bf16[64,4096]{1,0:T(8,128)(2,1)}, bf16[8,512]{1,0:T(8,128)(2,1)}, bf16[8,512]{1,0:T(8,128)(2,1)}) custom-call(bf16[64,4096]{1,0:T(8,128)(2,1)S(1)} %get-tuple-element.7.att_in, bf16[64,4096]{1,0:T(8,128)(2,1)S(1)} %get-tuple-element.8.dq_in, bf16[8,4,16,128]{3,2,1,0:T(8,128)(2,1)S(1)} %get-tuple-element.9.landb), custom_call_target="tpu_custom_call" | custom-call | tf_op jit(solution)/shard_map/finish/pallas_call | solution.py:358
